TPU v7x, 256 devices: a whole 4x4x8 slice. The times are simulated.
256 devices in a mesh: lat: 64 (over z, x_hi, y), lon: 4 (over x_lo, core).
Axes of the slice: x: 4 (x_hi: 2, x_lo: 2; x = x_hi * 2 + x_lo), y: 4, z: 8, core: 2. Of those that a mesh axis runs over, the one named last changes fastest.
Arguments:
- field: bfloat16 [256, 1920, 256], P('lat', 'lon'), may hold values from -6 to 6
- filter_blocks: bfloat16 [256, 9, 5, 128], P('lat'), may hold values from -0.3125 to 0.3125
- filter_scales: float32 [256, 9], P('lat'), may hold values from 0.3 to 3
- lon_offsets: int32 [256], P('lat'), may hold values from -64 to 63, as said below
- lon_widths: int32 [256], P('lat'), may hold values from 1 to 128
- halo_rows: int32 [256], P('lat'), may hold values from 1 to 2
- mixing: bfloat16 [2304, 256], replicated, may hold values from -0.125 to 0.125
Outputs:
- mixed: bfloat16 [256, 1920, 256], P('lat', 'lon')
Inputs may be any that keep to these rules, and one draw needn't show every extreme that they name: lon_offsets[i] >= -64 and lon_offsets[i] + lon_widths[i] <= 64.
All inputs are finite; a program needn't handle non-finite values.
Results may differ from a plain program's by a relative error of at most 0.0049.
Values may be sent and summed in bfloat16 or wider, within the bound.
A program may use at most 192 MiB of HBM per device.

v0:
```python
import jax
import jax.numpy as jnp
from jax import lax
from jax.sharding import PartitionSpec as P

BASIS = 9
HROWS = 2
REACH = 64
BLOCK = 120


def with_halo(cells, sides, width, closed):
    for axis, dim in sides:
        count = lax.axis_size(axis)
        ends = count if closed else count - 1
        head = lax.slice_in_dim(cells, 0, width, axis=dim)
        tail = lax.slice_in_dim(cells, cells.shape[dim] - width, cells.shape[dim], axis=dim)
        cells = jnp.concatenate(
            [
                lax.ppermute(tail, axis, [(i, (i + 1) % count) for i in range(ends)]),
                cells,
                lax.ppermute(head, axis, [((i + 1) % count, i) for i in range(ends)]),
            ],
            axis=dim,
        )
    return cells


def make_band(block, offset, width, hrow):
    cols = jnp.arange(BLOCK, dtype=jnp.int32)[None, :, None]
    inputs = jnp.arange(BLOCK + 2 * REACH, dtype=jnp.int32)[None, None, :]
    entries = jnp.arange(2 * REACH, dtype=jnp.int32)[:, None, None]
    entry = inputs - cols - REACH - offset
    selector = ((entry == entries) & (entries < width)).astype(jnp.bfloat16)
    taps = jnp.abs(jnp.arange(2 * HROWS + 1, dtype=jnp.int32) - HROWS) <= hrow
    masked = jnp.where(taps[None, :, None], block, jnp.zeros_like(block))
    band = jnp.einsum("ktw,wjq->ktjq", masked, selector, preferred_element_type=jnp.float32)
    return band.astype(jnp.bfloat16)


def lon_extend(values):
    return with_halo(values, (("lon", 1),), REACH, True)


def lat_extend(values):
    return with_halo(values, (("lat", 0),), HROWS, False)


def on_device(field, filter_blocks, filter_scales, lon_offsets, lon_widths, halo_rows, mixing):
    lat_rows, lon_cols, chans = field.shape
    extended = lat_extend(lon_extend(field))
    bands = jax.vmap(make_band)(filter_blocks, lon_offsets, lon_widths, halo_rows)
    weights = mixing.reshape(BASIS, chans, mixing.shape[1])
    outputs = []
    for part in range(lon_cols // BLOCK):
        window = extended[:, part * BLOCK : part * BLOCK + BLOCK + 2 * REACH, :]
        summed = jnp.zeros((lat_rows, BASIS, BLOCK, chans), jnp.float32)
        for tap in range(2 * HROWS + 1):
            summed = summed + jnp.einsum(
                "ikjq,iqc->ikjc",
                bands[:, :, tap],
                window[tap : tap + lat_rows],
                preferred_element_type=jnp.float32,
            )
        conv = (summed * filter_scales[:, :, None, None]).astype(jnp.bfloat16)
        result = jnp.einsum("ikjc,kco->ijo", conv, weights, preferred_element_type=jnp.float32)
        outputs.append(result.astype(jnp.bfloat16))
    return jnp.concatenate(outputs, 1)


def solution(mesh):
    in_specs = (
        P("lat", "lon", None),
        P("lat", None, None, None),
        P("lat", None),
        P("lat"),
        P("lat"),
        P("lat"),
        P(),
    )
    out_specs = P("lat", "lon", None)
    return jax.shard_map(
        on_device, mesh=mesh, in_specs=in_specs, out_specs=out_specs, check_vma=False
    )
```

profile of v0, /device:TPU:124, one launch (start us, length us, event | category | flops | bytes accessed | tf_op | source)
XLA Modules:
  0.0 188.4 jit_solution(7462204881751009684)
XLA Ops:
  0.0 1.1 fusion.180
  1.2 1.7 collective-permute-start.1
  5.2 0.9 select_bitcast_fusion
  6.0 36.3 %fusion.6 = bf16[4,9,5,120,248]{4,2,3,1,0:T(8,128)(2,1)} fusion(s32[4,120,248]{2,1,0:T(8,128)S(1)} %broadcast_subtract_fusion, pred[4,128]{1,0:T(4,128)(4,1)S(1)} %iota_compare_fusion.1, bf16[4,9,5,128,1]{3,0,2,1,4:T(4,128)(2,1)S(1)} %select_bitcast_fusion), kind=kOutput, calls=%fused_computation.6 | convolution fusion | flops 1407171840 | bytes 11236352 | tf_op jit(solution)/shard_map/vmap(ktw,wjq->ktjq)/dot_general | solution.py:37
  42.3 36.7 %fusion.178 = (bf16[4,9,1,120,248]{4,2,3,1,0:T(2,128)(2,1)}, bf16[4,9,1,120,248]{4,2,3,1,0:T(2,128)(2,1)}, bf16[4,9,1,120,248]{4,2,3,1,0:T(2,128)(2,1)}, bf16[4,...) fusion(bf16[4,9,5,120,248]{4,2,3,1,0:T(8,128)(2,1)} %fusion.6), kind=kLoop, calls=%fused_computation.164 | loop fusion | bytes 21427200 | tf_op jit(solution)/shard_map/slice | solution.py:61
  79.0 2.8 %copy.40 = bf16[4,9,1,120,248]{4,3,2,1,0:T(8,128)(2,1)S(1)} copy(bf16[4,9,1,120,248]{4,2,3,1,0:T(2,128)(2,1)} %get-tuple-element.8) | data formatting | bytes 4285440
  81.8 2.9 %fusion.27 = f32[4,9,120,256]{3,2,1,0:T(8,128)} fusion(bf16[4,9,1,120,248]{4,3,2,1,0:T(8,128)(2,1)S(1)} %copy.40, bf16[4,480,256]{2,1,0:T(8,128)(2,1)S(1)} %copy-done.1), kind=kOutput, calls=%fused_computation.57 | convolution fusion | flops 548536320 | bytes 7143424 | tf_op jit(solution)/shard_map/ikjq,iqc->ikjc/dot_general | solution.py:59
  84.7 2.8 %fusion.29 = f32[4,9,120,256]{3,2,1,0:T(8,128)} fusion(bf16[4,9,1,120,248]{4,3,2,1,0:T(8,128)(2,1)S(1)} %copy.40, bf16[4,480,256]{2,1,0:T(8,128)(2,1)S(1)} %copy-done.1), kind=kOutput, calls=%fused_computation.59 | convolution fusion | flops 548536320 | bytes 7143424 | tf_op jit(solution)/shard_map/ikjq,iqc->ikjc/dot_general | solution.py:59
  89.1 0.9 slice-done
  90.1 1.8 copy.38
  92.0 2.7 %collective-permute-start.3 = (bf16[2,608,256]{2,1,0:T(8,128)(2,1)S(1)}, bf16[2,608,256]{2,1,0:T(8,128)(2,1)S(1)}, u32[]{:S(2)}, u32[]{:S(2)}) collective-permute-start(bf16[2,608,256]{2,1,0:T(8,128)(2,1)S(1)} %get-tuple-element.11), channel_id=1, source_target_pairs={{4,0},{8,4},{12,8},{16,12},{20,16},{24,20},{28,24},{32,28},{36,32}... | collective-permute-start | bytes 1867784 | tf_op jit(solution)/shard_map/ppermute | solution.py:22
  94.7 9.1 %collective-permute-start.2 = (bf16[2,608,256]{2,1,0:T(8,128)(2,1)S(1)}, bf16[2,608,256]{2,1,0:T(8,128)(2,1)S(1)}, u32[]{:S(2)}, u32[]{:S(2)}) collective-permute-start(bf16[2,608,256]{2,1,0:T(8,128)(2,1)S(1)} %get-tuple-element.10), channel_id=1, source_target_pairs={{0,4},{4,8},{8,12},{12,16},{16,20},{20,24},{24,28},{28,32},{32,36}... | collective-permute-start | bytes 1867784 | tf_op jit(solution)/shard_map/ppermute | solution.py:20
  103.8 2.8 %fusion.25 = f32[4,9,120,256]{3,2,1,0:T(8,128)} fusion(bf16[4,9,1,120,248]{4,3,2,1,0:T(8,128)(2,1)S(1)} %copy.40, bf16[4,64,256]{2,1,0:T(8,128)(2,1)S(1)} %collective-permute-done.1, bf16[4,480,256]{2,1,0:T(8,128)(2,1)S(1)} %copy-done.1), kind=kOutput, calls=%fused_computation.55 | convolution fusion | flops 549552128 | bytes 7680512 | tf_op jit(solution)/shard_map/ikjq,iqc->ikjc/dot_general | solution.py:59
  106.5 2.8 %fusion.31 = f32[4,9,120,256]{3,2,1,0:T(8,128)} fusion(bf16[4,9,1,120,248]{4,3,2,1,0:T(8,128)(2,1)S(1)} %copy.40, bf16[4,480,256]{2,1,0:T(8,128)(2,1)S(1)} %copy-done.1, bf16[4,64,256]{2,1,0:T(8,128)(2,1)S(1)} %collective-permute-done), kind=kOutput, calls=%fused_computation.61 | convolution fusion | flops 549552128 | bytes 7680512 | tf_op jit(solution)/shard_map/ikjq,iqc->ikjc/dot_general | solution.py:59
  109.4 5.8 %collective-permute-done.3 = bf16[2,608,256]{2,1,0:T(8,128)(2,1)S(1)} collective-permute-done((bf16[2,608,256]{2,1,0:T(8,128)(2,1)S(1)}, bf16[2,608,256]{2,1,0:T(8,128)(2,1)S(1)}, u32[]{:S(2)}, u32[]{:S(2)}) %collective-permute-start.3) | collective-permute-done | bytes 622624 | tf_op jit(solution)/shard_map/ppermute | solution.py:22
  115.2 2.8 %fusion.9 = f32[4,9,120,256]{3,2,1,0:T(8,128)} fusion(bf16[4,9,1,120,248]{4,3,2,1,0:T(8,128)(2,1)S(1)} %copy.42, bf16[2,608,256]{2,1,0:T(8,128)(2,1)S(1)} %collective-permute-done.3, bf16[4,608,256]{2,1,0:T(8,128)(2,1)S(1)} %constant_dynamic-update-slice_fusion), kind=kOutput, calls=%fused_computation.39 | convolution fusion | flops 549552128 | bytes 8434176 | tf_op jit(solution)/shard_map/ikjq,iqc->ikjc/dot_general | solution.py:59
  117.9 2.9 %fusion.11 = f32[4,9,120,256]{3,2,1,0:T(8,128)} fusion(bf16[4,9,1,120,248]{4,3,2,1,0:T(8,128)(2,1)S(1)} %copy.42, bf16[4,608,256]{2,1,0:T(8,128)(2,1)S(1)} %constant_dynamic-update-slice_fusion, bf16[2,608,256]{2,1,0:T(8,128)(2,1)S(1)} %collective-permute-done.3), kind=kOutput, calls=%fused_computation.41 | convolution fusion | flops 548790272 | bytes 8434176 | tf_op jit(solution)/shard_map/ikjq,iqc->ikjc/dot_general | solution.py:59
  120.8 2.7 %fusion.17 = f32[4,9,120,256]{3,2,1,0:T(8,128)} fusion(bf16[4,9,1,120,248]{4,3,2,1,0:T(8,128)(2,1)S(1)} %copy.41, bf16[4,608,256]{2,1,0:T(8,128)(2,1)S(1)} %constant_dynamic-update-slice_fusion, bf16[2,608,256]{2,1,0:T(8,128)(2,1)S(1)} %collective-permute-done.3), kind=kOutput, calls=%fused_computation.47 | convolution fusion | flops 548790272 | bytes 8434176 | tf_op jit(solution)/shard_map/ikjq,iqc->ikjc/dot_general | solution.py:59
  123.5 2.9 %fusion.19 = f32[4,9,120,256]{3,2,1,0:T(8,128)} fusion(bf16[4,9,1,120,248]{4,3,2,1,0:T(8,128)(2,1)S(1)} %copy.41, bf16[4,608,256]{2,1,0:T(8,128)(2,1)S(1)} %constant_dynamic-update-slice_fusion, bf16[2,608,256]{2,1,0:T(8,128)(2,1)S(1)} %collective-permute-done.3), kind=kOutput, calls=%fused_computation.49 | convolution fusion | flops 548790272 | bytes 8434176 | tf_op jit(solution)/shard_map/ikjq,iqc->ikjc/dot_general | solution.py:59
  126.5 2.8 %fusion.33 = f32[4,9,120,256]{3,2,1,0:T(8,128)} fusion(bf16[4,9,1,120,248]{4,3,2,1,0:T(8,128)(2,1)S(1)} %copy.39, bf16[4,608,256]{2,1,0:T(8,128)(2,1)S(1)} %constant_dynamic-update-slice_fusion, bf16[2,608,256]{2,1,0:T(8,128)(2,1)S(1)} %collective-permute-done.2), kind=kOutput, calls=%fused_computation.63 | convolution fusion | flops 549552128 | bytes 8434176 | tf_op jit(solution)/shard_map/ikjq,iqc->ikjc/dot_general | solution.py:59
  129.2 2.8 %fusion.35 = f32[4,9,120,256]{3,2,1,0:T(8,128)} fusion(bf16[4,9,1,120,248]{4,3,2,1,0:T(8,128)(2,1)S(1)} %copy.39, bf16[4,608,256]{2,1,0:T(8,128)(2,1)S(1)} %constant_dynamic-update-slice_fusion, bf16[2,608,256]{2,1,0:T(8,128)(2,1)S(1)} %collective-permute-done.2), kind=kOutput, calls=%fused_computation.65 | convolution fusion | flops 548790272 | bytes 8434176 | tf_op jit(solution)/shard_map/ikjq,iqc->ikjc/dot_general | solution.py:59
  132.0 2.8 %fusion.13 = f32[4,9,120,256]{3,2,1,0:T(8,128)} fusion(bf16[4,9,1,120,248]{4,3,2,1,0:T(8,128)(2,1)S(1)} %copy.42, bf16[4,608,256]{2,1,0:T(8,128)(2,1)S(1)} %constant_dynamic-update-slice_fusion, bf16[2,608,256]{2,1,0:T(8,128)(2,1)S(1)} %collective-permute-done.3), kind=kOutput, calls=%fused_computation.43 | convolution fusion | flops 548790272 | bytes 8434176 | tf_op jit(solution)/shard_map/ikjq,iqc->ikjc/dot_general | solution.py:59
  134.8 2.8 %fusion.21 = f32[4,9,120,256]{3,2,1,0:T(8,128)} fusion(bf16[4,9,1,120,248]{4,3,2,1,0:T(8,128)(2,1)S(1)} %copy.41, bf16[4,608,256]{2,1,0:T(8,128)(2,1)S(1)} %constant_dynamic-update-slice_fusion, bf16[2,608,256]{2,1,0:T(8,128)(2,1)S(1)} %collective-permute-done.3), kind=kOutput, calls=%fused_computation.51 | convolution fusion | flops 548790272 | bytes 8434176 | tf_op jit(solution)/shard_map/ikjq,iqc->ikjc/dot_general | solution.py:59
  137.6 2.8 %fusion.37 = f32[4,9,120,256]{3,2,1,0:T(8,128)} fusion(bf16[4,9,1,120,248]{4,3,2,1,0:T(8,128)(2,1)S(1)} %copy.39, bf16[4,608,256]{2,1,0:T(8,128)(2,1)S(1)} %constant_dynamic-update-slice_fusion, bf16[2,608,256]{2,1,0:T(8,128)(2,1)S(1)} %collective-permute-done.2), kind=kOutput, calls=%fused_computation.67 | convolution fusion | flops 548790272 | bytes 8434176 | tf_op jit(solution)/shard_map/ikjq,iqc->ikjc/dot_general | solution.py:59
  140.4 2.8 %fusion.15 = f32[4,9,120,256]{3,2,1,0:T(8,128)} fusion(bf16[4,9,1,120,248]{4,3,2,1,0:T(8,128)(2,1)S(1)} %copy.42, bf16[4,608,256]{2,1,0:T(8,128)(2,1)S(1)} %constant_dynamic-update-slice_fusion, bf16[2,608,256]{2,1,0:T(8,128)(2,1)S(1)} %collective-permute-done.3), kind=kOutput, calls=%fused_computation.45 | convolution fusion | flops 548790272 | bytes 8434176 | tf_op jit(solution)/shard_map/ikjq,iqc->ikjc/dot_general | solution.py:59
  143.2 2.8 %fusion.23 = f32[4,9,120,256]{3,2,1,0:T(8,128)} fusion(bf16[4,9,1,120,248]{4,3,2,1,0:T(8,128)(2,1)S(1)} %copy.41, bf16[4,608,256]{2,1,0:T(8,128)(2,1)S(1)} %constant_dynamic-update-slice_fusion, bf16[2,608,256]{2,1,0:T(8,128)(2,1)S(1)} %collective-permute-done.3), kind=kOutput, calls=%fused_computation.53 | convolution fusion | flops 548790272 | bytes 8434176 | tf_op jit(solution)/shard_map/ikjq,iqc->ikjc/dot_general | solution.py:59
  146.0 2.8 %fusion.39 = f32[4,9,120,256]{3,2,1,0:T(8,128)} fusion(bf16[4,9,1,120,248]{4,3,2,1,0:T(8,128)(2,1)S(1)} %copy.39, bf16[4,608,256]{2,1,0:T(8,128)(2,1)S(1)} %constant_dynamic-update-slice_fusion, bf16[2,608,256]{2,1,0:T(8,128)(2,1)S(1)} %collective-permute-done.2), kind=kOutput, calls=%fused_computation.69 | convolution fusion | flops 548790272 | bytes 8434176 | tf_op jit(solution)/shard_map/ikjq,iqc->ikjc/dot_general | solution.py:59
  148.8 9.0 %fusion.90 = bf16[4,120,256]{2,1,0:T(8,128)(2,1)S(1)} fusion(bf16[9,256,256,1]{2,1,0,3:T(8,128)(2,1)S(1)} %bitcast.222, f32[4,9,120,256]{3,2,1,0:T(8,128)} %fusion.9, f32[4,9,120,256]{3,2,1,0:T(8,128)} %fusion.17, f32[4,9,120,256]{3,2,1,0:T(8,128)} %fusion.25, f32[4,9,120,256]{3,2,1,0:T(8,128)} %fusion.33, f32[4,9]{1,0:T(4,128)S(1)} %copy-done.2, ...), kind=kOutput, calls=%fused_computation.90 | convolution fusion | flops 1121779712 | bytes 23130768 | tf_op jit(solution)/shard_map/ikjc,kco->ijo/dot_general | solution.py:66
  157.8 9.2 %fusion.87 = bf16[4,120,256]{2,1,0:T(8,128)(2,1)S(1)} fusion(bf16[9,256,256,1]{2,1,0,3:T(8,128)(2,1)S(1)} %bitcast.221, f32[4,9,120,256]{3,2,1,0:T(8,128)} %fusion.11, f32[4,9,120,256]{3,2,1,0:T(8,128)} %fusion.19, f32[4,9,120,256]{3,2,1,0:T(8,128)} %fusion.27, f32[4,9,120,256]{3,2,1,0:T(8,128)} %fusion.35, f32[4,9]{1,0:T(4,128)S(1)} %copy-done.2, ...), kind=kOutput, calls=%fused_computation.89 | convolution fusion | flops 1121779712 | bytes 23130768 | tf_op jit(solution)/shard_map/ikjc,kco->ijo/dot_general | solution.py:66
  167.0 9.7 %fusion.84 = bf16[4,120,256]{2,1,0:T(8,128)(2,1)} fusion(bf16[9,256,256,1]{2,1,0,3:T(8,128)(2,1)S(1)} %bitcast.220, f32[4,9,120,256]{3,2,1,0:T(8,128)} %fusion.13, f32[4,9,120,256]{3,2,1,0:T(8,128)} %fusion.21, f32[4,9,120,256]{3,2,1,0:T(8,128)} %fusion.29, f32[4,9,120,256]{3,2,1,0:T(8,128)} %fusion.37, f32[4,9]{1,0:T(4,128)S(1)} %copy-done.2, ...), kind=kOutput, calls=%fused_computation.88 | convolution fusion | flops 1121779712 | bytes 23130768 | tf_op jit(solution)/shard_map/ikjc,kco->ijo/dot_general | solution.py:66
  176.7 9.7 %fusion.81 = bf16[4,120,256]{2,1,0:T(8,128)(2,1)} fusion(bf16[9,256,256,1]{2,1,0,3:T(8,128)(2,1)S(1)} %bitcast.219, f32[4,9,120,256]{3,2,1,0:T(8,128)} %fusion.15, f32[4,9,120,256]{3,2,1,0:T(8,128)} %fusion.23, f32[4,9,120,256]{3,2,1,0:T(8,128)} %fusion.31, f32[4,9,120,256]{3,2,1,0:T(8,128)} %fusion.39, f32[4,9]{1,0:T(4,128)S(1)} %copy-done.2, ...), kind=kOutput, calls=%fused_computation.87 | convolution fusion | flops 1121779712 | bytes 23130768 | tf_op jit(solution)/shard_map/ikjc,kco->ijo/dot_general | solution.py:66
  186.4 2.1 %pad_maximum_fusion = bf16[4,480,256]{2,1,0:T(8,128)(2,1)} fusion(bf16[4,120,256]{2,1,0:T(8,128)(2,1)S(1)} %fusion.90, bf16[4,120,256]{2,1,0:T(8,128)(2,1)S(1)} %fusion.87, bf16[4,120,256]{2,1,0:T(8,128)(2,1)} %fusion.84, bf16[4,120,256]{2,1,0:T(8,128)(2,1)} %fusion.81), kind=kLoop, calls=%fused_computation.91 | loop fusion | flops 3932160 | bytes 1966080 | tf_op jit(solution)/shard_map/concatenate | solution.py:68
  (41 shorter events, 4.0 us)
Async XLA Ops:
  0.0 148.8 %copy-start = (bf16[2304,256]{1,0:T(8,128)(2,1)S(1)}, bf16[2304,256]{1,0:T(8,128)(2,1)}, u32[]{:S(2)}) copy-start(bf16[2304,256]{1,0:T(8,128)(2,1)} %param.13) | copy-start | bytes 3538948
  1.1 90.7 %collective-permute-start = (bf16[4,64,256]{2,1,0:T(8,128)(2,1)S(1)}, bf16[4,64,256]{2,1,0:T(8,128)(2,1)S(1)}, u32[]{:S(2)}, u32[]{:S(2)}) collective-permute-start(bf16[4,64,256]{2,1,0:T(8,128)(2,1)S(1)} %get-tuple-element.13), channel_id=1, source_target_pairs={{0,1},{1,2},{2,3},{3,0},{4,5},{5,6},{6,7},{7,4},{8,9},{9,10},{10,1... | collective-permute-start | bytes 393224 | tf_op jit(solution)/shard_map/ppermute | solution.py:20
  1.2 90.7 %collective-permute-start.1 = (bf16[4,64,256]{2,1,0:T(8,128)(2,1)S(1)}, bf16[4,64,256]{2,1,0:T(8,128)(2,1)S(1)}, u32[]{:S(2)}, u32[]{:S(2)}) collective-permute-start(bf16[4,64,256]{2,1,0:T(8,128)(2,1)S(1)} %get-tuple-element.12), channel_id=1, source_target_pairs={{1,0},{2,1},{3,2},{0,3},{5,4},{6,5},{7,6},{4,7},{9,8},{10,9},{11,1... | collective-permute-start | bytes 393224 | tf_op jit(solution)/shard_map/ppermute | solution.py:22
  79.0 2.8 %copy-start.1 = (bf16[4,480,256]{2,1,0:T(8,128)(2,1)S(1)}, bf16[4,480,256]{2,1,0:T(8,128)(2,1)}, u32[]{:S(2)}) copy-start(bf16[4,480,256]{2,1,0:T(8,128)(2,1)} %param.7) | copy-start | bytes 2949124
  79.0 8.6 %slice-start.6 = ((s8[4423680]{0:T(1024)(128)(4,1)}), s8[4194304]{0:T(1024)(128)(4,1)S(1)}, s32[]{:S(2)}) async-start(s8[4423680]{0:T(1024)(128)(4,1)} %bitcast.229), calls=%async_computation.6 | async-start | bytes 8388608
  81.8 5.7 %slice-start.7 = ((s8[4423680]{0:T(1024)(128)(4,1)}), s8[229376]{0:T(1024)(128)(4,1)S(1)}, s32[]{:S(2)}) async-start(s8[4423680]{0:T(1024)(128)(4,1)} %bitcast.229), calls=%async_computation.7 | async-start | bytes 458752
  81.8 6.1 %slice-start.4 = ((s8[4423680]{0:T(1024)(128)(4,1)}), s8[4194304]{0:T(1024)(128)(4,1)S(1)}, s32[]{:S(2)}) async-start(s8[4423680]{0:T(1024)(128)(4,1)} %bitcast.227), calls=%async_computation.4 | async-start | bytes 8388608
  84.7 3.3 %slice-start.5 = ((s8[4423680]{0:T(1024)(128)(4,1)}), s8[229376]{0:T(1024)(128)(4,1)S(1)}, s32[]{:S(2)}) async-start(s8[4423680]{0:T(1024)(128)(4,1)} %bitcast.227), calls=%async_computation.5 | async-start | bytes 458752
  84.7 3.8 %slice-start.2 = ((s8[4423680]{0:T(1024)(128)(4,1)}), s8[4194304]{0:T(1024)(128)(4,1)S(1)}, s32[]{:S(2)}) async-start(s8[4423680]{0:T(1024)(128)(4,1)} %bitcast.225), calls=%async_computation.2 | async-start | bytes 8388608
  87.6 1.2 slice-start.3
  87.6 2.5 %slice-start = ((s8[4423680]{0:T(1024)(128)(4,1)}), s8[4194304]{0:T(1024)(128)(4,1)S(1)}, s32[]{:S(2)}) async-start(s8[4423680]{0:T(1024)(128)(4,1)} %bitcast.223), calls=%async_computation | async-start | bytes 8388608
  88.0 2.1 %slice-start.1 = ((s8[4423680]{0:T(1024)(128)(4,1)}), s8[229376]{0:T(1024)(128)(4,1)S(1)}, s32[]{:S(2)}) async-start(s8[4423680]{0:T(1024)(128)(4,1)} %bitcast.223), calls=%async_computation.1 | async-start | bytes 458752
  92.0 23.1 %collective-permute-start.3 = (bf16[2,608,256]{2,1,0:T(8,128)(2,1)S(1)}, bf16[2,608,256]{2,1,0:T(8,128)(2,1)S(1)}, u32[]{:S(2)}, u32[]{:S(2)}) collective-permute-start(bf16[2,608,256]{2,1,0:T(8,128)(2,1)S(1)} %get-tuple-element.11), channel_id=1, source_target_pairs={{4,0},{8,4},{12,8},{16,12},{20,16},{24,20},{28,24},{32,28},{36,32}... | collective-permute-start | bytes 1867784 | tf_op jit(solution)/shard_map/ppermute | solution.py:22
  94.7 31.8 %collective-permute-start.2 = (bf16[2,608,256]{2,1,0:T(8,128)(2,1)S(1)}, bf16[2,608,256]{2,1,0:T(8,128)(2,1)S(1)}, u32[]{:S(2)}, u32[]{:S(2)}) collective-permute-start(bf16[2,608,256]{2,1,0:T(8,128)(2,1)S(1)} %get-tuple-element.10), channel_id=1, source_target_pairs={{0,4},{4,8},{8,12},{12,16},{16,20},{20,24},{24,28},{28,32},{32,36}... | collective-permute-start | bytes 1867784 | tf_op jit(solution)/shard_map/ppermute | solution.py:20
  146.0 2.8 %copy-start.2 = (f32[4,9]{1,0:T(4,128)S(1)}, f32[4,9]{1,0:T(4,128)}, u32[]{:S(2)}) copy-start(f32[4,9]{1,0:T(4,128)} %param.9) | copy-start | bytes 436
where the time goes:
time: 189 us; the launch traced here: 188 us
  matrix products  119 us (63%)
  local copies, waits for them, and re-layouts  44.9 us (24%)
  starting transfers between devices  13.6 us (7%)
  waiting for transfers between devices  5.79 us (3%)
  other arithmetic  5.18 us (3%)
    dot_general x16, matrix products, on_device(): jnp.einsum('ikjq,iqc->ikjc', bands[:, :, tap], window[tap:tap + lat_rows]...  44.9 us
    dot_general x4, matrix products, on_device(): jnp.einsum('ikjc,kco->ijo', conv, weights, preferred_element_type=jnp.flo...  37.5 us
    slice x1, local copies, waits for them, and re-layouts, on_device(): bands[:, :, tap]  36.7 us
    dot_general x1, matrix products, make_band(): jnp.einsum('ktw,wjq->ktjq', masked, selector, preferred_element_type=jnp....  36.3 us
    ppermute x2, starting transfers between devices, with_halo(): lax.ppermute(tail, axis, [(i, (i + 1) % count) for i in range(ends)])  9.18 us
    unnamed x29, local copies, waits for them, and re-layouts  7.08 us
    ppermute x2, waiting for transfers between devices, with_halo(): lax.ppermute(head, axis, [((i + 1) % count, i) for i in range(ends)])  5.78 us
    ppermute x2, starting transfers between devices, with_halo(): lax.ppermute(head, axis, [((i + 1) % count, i) for i in range(ends)])  4.38 us
  transfers between devices with their start and end apart: 4, of which 1 were waited for; matrix products, arithmetic and copies ran while one was open for 55% of the time, Pallas kernels for 0%

commit v1 on v0

v1 whole, which is shorter than its diff:
```python
import functools

import jax
import jax.numpy as jnp
from jax import lax
from jax.experimental import pallas as pl
from jax.experimental.pallas import tpu as pltpu
from jax.sharding import PartitionSpec as P

MESH = pl.DeviceIdType.MESH
BASIS = 9
TAPS = 5
HROWS = 2
REACH = 64
SPAN = 2 * REACH
BLOCK = 32
GROUP = 5
F32 = jnp.float32
BF16 = jnp.bfloat16

OWN_TAPS = ((2, 3, 4), (1, 2, 3, 4), (0, 1, 2, 3), (0, 1, 2))
AWAY_TAPS = ((0, 1), (0,), (4,), (3, 4))


def kernel(
    n_lat, n_lon,
    x_ref, f_ref, s_ref, off_ref, wid_ref, halo_ref, w_hbm, out,
    ext, lines, moved, a_own, a_away, acc, conv, tail, w_ref,
    own_sem, near_s, near_r, far_s, far_r, lon_s, lon_r, rel_s, rel_r,
):
    rows, cols, chans = x_ref.shape
    la, lo = lax.axis_index("lat"), lax.axis_index("lon")
    west, east = lax.rem(lo + n_lon - 1, n_lon), lax.rem(lo + 1, n_lon)
    has_n, has_s = la > 0, la < n_lat - 1
    far_cuts = ((0, 64), (cols - 64, 64), (64, 160), (224, 160), (384, 32))

    barrier = pltpu.get_barrier_semaphore()
    for lon in (west, east):
        pl.semaphore_signal(barrier, inc=1, device_id=(la, lon), device_id_type=MESH)

    @pl.when(has_n)
    def _():
        pl.semaphore_signal(barrier, inc=1, device_id=(la - 1, lo), device_id_type=MESH)

    @pl.when(has_s)
    def _():
        pl.semaphore_signal(barrier, inc=1, device_id=(la + 1, lo), device_id_type=MESH)

    own = pltpu.make_async_copy(
        x_ref, ext.at[pl.ds(HROWS, rows), pl.ds(REACH, cols)], own_sem.at[0]
    )
    own.start()
    weights = pltpu.make_async_copy(w_hbm, w_ref, own_sem.at[1])
    weights.start()

    peers = 2 + jnp.where(has_n, 1, 0) + jnp.where(has_s, 1, 0)
    pl.semaphore_wait(barrier, peers)

    def near_copy(d):
        src, dst, to = ((rows - 1, 1, la + 1), (0, rows + HROWS, la - 1))[d]
        return pltpu.make_async_remote_copy(
            x_ref.at[src], ext.at[dst, pl.ds(REACH, cols)],
            near_s.at[d], near_r.at[d], device_id=(to, lo), device_id_type=MESH,
        )

    def far_copy(d, p):
        src, dst, to = ((rows - 2, 0, la + 1), (1, rows + HROWS + 1, la - 1))[d]
        at, size = far_cuts[p]
        return pltpu.make_async_remote_copy(
            x_ref.at[src, pl.ds(at, size)], ext.at[dst, pl.ds(REACH + at, size)],
            far_s.at[d, p], far_r.at[d, p], device_id=(to, lo), device_id_type=MESH,
        )

    def lon_copy(d):
        at, to, land = ((cols - REACH, east, 0), (0, west, cols + REACH))[d]
        return pltpu.make_async_remote_copy(
            x_ref.at[:, pl.ds(at, REACH)], ext.at[pl.ds(HROWS, rows), pl.ds(land, REACH)],
            lon_s.at[d], lon_r.at[d], device_id=(la, to), device_id_type=MESH,
        )

    def relay(r, d):
        row = (1, rows + HROWS, 0, rows + HROWS + 1)[r]
        at, to, land = ((cols, east, 0), (REACH, west, cols + REACH))[d]
        return pltpu.make_async_remote_copy(
            ext.at[row, pl.ds(at, REACH)], ext.at[row, pl.ds(land, REACH)],
            rel_s.at[r, d], rel_r.at[r, d], device_id=(la, to), device_id_type=MESH,
        )

    sends = (has_s, has_n)
    comes = (has_n, has_s)
    pieces = range(len(far_cuts))

    for d in range(2):
        @pl.when(sends[d])
        def _():
            near_copy(d).start()

    for d in range(2):
        lon_copy(d).start()

    for d in range(2):
        @pl.when(sends[d])
        def _():
            for p in pieces:
                far_copy(d, p).start()

    @pl.when(jnp.logical_not(has_n))
    def _():
        ext[0:HROWS] = jnp.zeros((HROWS, cols + SPAN, chans), BF16)

    @pl.when(jnp.logical_not(has_s))
    def _():
        ext[rows + HROWS:] = jnp.zeros((HROWS, cols + SPAN, chans), BF16)

    tall = BASIS * BLOCK
    lane = lax.broadcasted_iota(jnp.int32, (BLOCK, SPAN), 1)
    step = lax.broadcasted_iota(jnp.int32, (BLOCK, SPAN), 0)
    entry = lax.broadcasted_iota(jnp.int32, (SPAN, SPAN), 0)
    place = lax.broadcasted_iota(jnp.int32, (SPAN, SPAN), 1)
    n_lines = lines.shape[0]
    line_at = lax.broadcasted_iota(jnp.int32, (n_lines, SPAN), 0)
    line_tap = (line_at - line_at // (TAPS * rows) * (TAPS * rows)) // rows

    lines[n_lines - 8:] = jnp.zeros((8, SPAN), F32)
    for k in range(BASIS):
        for t in range(TAPS):
            at = (k * TAPS + t) * rows
            lines[at:at + rows] = f_ref[k, t].astype(F32)
    for i in range(rows):
        hit = (place == entry + off_ref[i] + REACH) & (entry < wid_ref[i])
        mover = jnp.where(hit, 1.0, 0.0).astype(BF16)
        shifted = jnp.dot(lines[...].astype(BF16), mover, preferred_element_type=F32)
        moved[i] = jnp.where(jnp.abs(line_tap - HROWS) <= halo_ref[i], shifted, 0.0)

    def unit(ref, i, j, k, taps):
        at = k * BLOCK
        rest = jnp.zeros((BLOCK, SPAN), F32)
        for u, t in enumerate(taps):
            row = (k * TAPS + t) * rows + i
            line = jnp.broadcast_to(moved[i, row:row + 1], (BLOCK, SPAN))
            skew = pltpu.roll(line, 0, 1, stride=1, stride_axis=0)
            head = jnp.where(lane >= step, skew, 0.0)
            ref[j, at:at + BLOCK, u * SPAN:(u + 1) * SPAN] = head.astype(BF16)
            spot = lane - u * BLOCK
            turned = pltpu.roll(skew, u * BLOCK, 1) if u else skew
            rest = jnp.where((spot >= 0) & (spot < step), turned, rest)
        n = len(taps)
        ref[j, at:at + BLOCK, n * SPAN:(n + 1) * SPAN] = rest.astype(BF16)

    def window(rows_in, b):
        at = b * BLOCK
        heads = [ext[r, at:at + SPAN] for r in rows_in]
        rests = [ext[r, at + SPAN:at + SPAN + BLOCK] for r in rows_in]
        return jnp.concatenate(heads + rests, 0)

    def part(ref, i, taps, b):
        depth = len(taps) * (SPAN + BLOCK)
        return jnp.dot(
            ref[i, :, 0:depth], window([i + t for t in taps], b), preferred_element_type=F32
        )

    def own_part(i, b):
        acc[i, b] = part(a_own, i, OWN_TAPS[i], b)

    def finish(i, b, ref, slot, at):
        total = acc[i, b] + part(a_away, i, AWAY_TAPS[i], b)
        for k in range(BASIS):
            scaled = total[k * BLOCK:(k + 1) * BLOCK] * s_ref[i, k]
            ref[slot, at:at + BLOCK, k * chans:(k + 1) * chans] = scaled.astype(BF16)

    blocks = cols // BLOCK
    for i in range(rows):
        for k in range(BASIS):
            unit(a_own, i, i, k, OWN_TAPS[i])
            unit(a_away, i, i, k, AWAY_TAPS[i])
    own.wait()
    for d in range(2):
        lon_copy(d).wait_recv()
    for b in range(blocks):
        own_part(1, b)
        own_part(2, b)

    def pass_on(d, r, waits):
        @pl.when(comes[d])
        def _():
            waits()
            for e in range(2):
                relay(r, e).start()

    def wait_relay(d, r):
        @pl.when(comes[d])
        def _():
            for e in range(2):
                relay(r, e).wait_recv()

    for d in range(2):
        pass_on(d, d, lambda: near_copy(d).wait_recv())
    for b in range(blocks):
        own_part(0, b)
        own_part(3, b)
    weights.wait()
    for d in range(2):
        wait_relay(d, d)
    for b in range(blocks):
        finish(1, b, conv, 0, b * BLOCK)
        finish(2, b, conv, 1, b * BLOCK)

    def edges(d):
        far_copy(d, 0).wait_recv()
        far_copy(d, 1).wait_recv()

    for d in range(2):
        pass_on(d, 2 + d, lambda: edges(d))
    for i in (1, 2):
        out[i] = jnp.dot(conv[i - 1], w_ref[...], preferred_element_type=F32).astype(BF16)

    for d in range(2):
        wait_relay(d, 2 + d)
    size = GROUP * BLOCK
    half = 4 * chans
    for g in range(blocks // GROUP):
        for d in range(2):
            @pl.when(comes[d])
            def _():
                far_copy(d, 2 + g).wait_recv()
        for u in range(GROUP):
            finish(0, g * GROUP + u, tail, 0, u * BLOCK)
            finish(3, g * GROUP + u, tail, 1, u * BLOCK)
        both = tail[...].reshape(2 * size, BASIS * chans)
        result = jnp.dot(both[:, :half], w_ref[:half], preferred_element_type=F32)
        result += jnp.dot(both[:, half:], w_ref[half:], preferred_element_type=F32)
        out[0, g * size:(g + 1) * size] = result[:size].astype(BF16)
        out[3, g * size:(g + 1) * size] = result[size:].astype(BF16)

    for d in range(2):
        @pl.when(sends[d])
        def _():
            near_copy(d).wait_send()
            for p in pieces:
                far_copy(d, p).wait_send()
    for d in range(2):
        lon_copy(d).wait_send()
    for d in range(2):
        @pl.when(comes[d])
        def _():
            for r in (d, 2 + d):
                for e in range(2):
                    relay(r, e).wait_send()


def hand_over(src, dst, sem):
    copy = pltpu.make_async_copy(src, dst, sem)
    copy.start()
    copy.wait()


def solution(mesh):
    n_lat, n_lon = mesh.shape["lat"], mesh.shape["lon"]

    def on_device(field, filter_blocks, filter_scales, lon_offsets, lon_widths, halo_rows, mixing):
        rows, cols, chans = field.shape
        outs = mixing.shape[1]
        wide = cols + SPAN
        blocks = cols // BLOCK
        tall = BASIS * BLOCK
        n_lines = -(-BASIS * TAPS * rows // 8) * 8
        smem = pl.BlockSpec(memory_space=pltpu.SMEM)
        hbm = pl.BlockSpec(memory_space=pl.ANY)
        dma = pltpu.SemaphoreType.DMA
        filters = jnp.transpose(filter_blocks, (1, 2, 0, 3))
        mixed = pl.pallas_call(
            functools.partial(kernel, n_lat, n_lon),
            out_shape=pltpu.VMEM((rows, cols, outs), BF16),
            in_specs=[hbm, pl.BlockSpec(memory_space=pltpu.VMEM), smem, smem, smem, smem, hbm],
            out_specs=pl.BlockSpec(memory_space=pltpu.VMEM),
            scratch_shapes=[
                pltpu.VMEM((rows + 2 * HROWS, wide, chans), BF16),
                pltpu.VMEM((n_lines, SPAN), F32),
                pltpu.VMEM((rows, n_lines, SPAN), F32),
                pltpu.VMEM((rows, tall, 5 * SPAN), BF16),
                pltpu.VMEM((rows, tall, 3 * SPAN), BF16),
                pltpu.VMEM((rows, blocks, tall, chans), F32),
                pltpu.VMEM((2, cols, BASIS * chans), BF16),
                pltpu.VMEM((2, GROUP * BLOCK, BASIS * chans), BF16),
                pltpu.VMEM((BASIS * chans, outs), BF16),
                dma((2,)),
                dma((2,)), dma((2,)),
                dma((2, 5)), dma((2, 5)),
                dma((2,)), dma((2,)),
                dma((4, 2)), dma((4, 2)),
            ],
            compiler_params=pltpu.CompilerParams(
                collective_id=0, has_side_effects=True, vmem_limit_bytes=56 * 2**20
            ),
            cost_estimate=pl.CostEstimate(
                flops=13_000_000_000, bytes_accessed=4_000_000, transcendentals=0
            ),
            name="disco",
        )(field, filters, filter_scales, lon_offsets, lon_widths, halo_rows, mixing)

        return pl.pallas_call(
            hand_over,
            out_shape=jax.ShapeDtypeStruct(mixed.shape, mixed.dtype),
            in_specs=[pl.BlockSpec(memory_space=pltpu.VMEM)],
            out_specs=hbm,
            scratch_shapes=[dma],
            name="hand_over",
        )(mixed)

    return jax.shard_map(
        on_device,
        mesh=mesh,
        in_specs=(
            P("lat", "lon", None),
            P("lat", None, None, None),
            P("lat", None),
            P("lat"),
            P("lat"),
            P("lat"),
            P(),
        ),
        out_specs=P("lat", "lon", None),
        check_vma=False,
    )
```

time: 189 us -> 41.4 us (0.22)
  the two profiles are of different devices: /device:TPU:124 before, /device:TPU:193 now
where the time goes in v1:
time: 41.4 us; the launch traced here: 41.2 us
  Pallas kernels  40.3 us (97%)
  local copies, waits for them, and re-layouts  0.94 us (2%)
    pallas_call x1, Pallas kernels, on_device(): pl.pallas_call(functools.partial(kernel, n_lat, n_lon), out_shape=pltpu.V...  38.1 us
    pallas_call x1, Pallas kernels, on_device(): pl.pallas_call(hand_over, out_shape=jax.ShapeDtypeStruct(mixed.shape, mix...  2.15 us
    unnamed x2, local copies, waits for them, and re-layouts  0.94 us

profile of v1, /device:TPU:193, one launch (start us, length us, event | category | flops | bytes accessed | tf_op | source)
XLA Modules:
  0.0 41.2 jit_solution(15870160904692945693)
XLA Ops:
  0.0 38.1 %disco.1.src = bf16[4,480,256]{2,1,0:T(8,128)(2,1)S(1)} custom-call(bf16[4,480,256]{2,1,0:T(8,128)(2,1)} %x_ref.1, bf16[9,5,4,128]{3,2,1,0:T(4,128)(2,1)} %bitcast.1, f32[4,9]{1,0:T(4,128)} %s_ref.1, s32[4]{0:T(128)} %off_ref.1, s32[4]{0:T(128)} %wid_ref.1, s32[4]{0:T(128)} %halo_ref.1, bf16[2304,256]{1,0:T(8,128)(2,1)} %w_hbm.1), custom_call_target="tpu_custom_call" | custom-call | flops 12999999488 | bytes 4000000 | tf_op jit(solution)/shard_map/disco/pallas_call | solution.py:271
  38.1 0.0 copy-start
  38.1 0.9 %copy-done = bf16[4,480,256]{2,1,0:T(8,128)(2,1)} copy-done((bf16[4,480,256]{2,1,0:T(8,128)(2,1)}, bf16[4,480,256]{2,1,0:T(8,128)(2,1)S(1)}, u32[]{:S(2)}) %copy-start) | copy-done | bytes 983064
  39.1 2.2 %hand_over.1 = bf16[4,480,256]{2,1,0:T(8,128)(2,1)} custom-call(bf16[4,480,256]{2,1,0:T(8,128)(2,1)} %copy-done), custom_call_target="tpu_custom_call" | custom-call | tf_op jit(solution)/shard_map/hand_over/pallas_call | solution.py:301
Async XLA Ops:
  38.1 1.0 %copy-start = (bf16[4,480,256]{2,1,0:T(8,128)(2,1)}, bf16[4,480,256]{2,1,0:T(8,128)(2,1)S(1)}, u32[]{:S(2)}) copy-start(bf16[4,480,256]{2,1,0:T(8,128)(2,1)S(1)} %disco.1.src) | copy-start | bytes 2949124

commit v2 on v1

v2 whole, which is shorter than its diff:
```python
import functools

import jax
import jax.numpy as jnp
from jax import lax
from jax.experimental import pallas as pl
from jax.experimental.pallas import tpu as pltpu
from jax.sharding import PartitionSpec as P

MESH = pl.DeviceIdType.MESH
BASIS = 9
TAPS = 5
HROWS = 2
REACH = 64
SPAN = 2 * REACH
BLOCK = 32
GROUP = 5
F32 = jnp.float32
BF16 = jnp.bfloat16

OWN_TAPS = ((2, 3, 4), (1, 2, 3, 4), (0, 1, 2, 3), (0, 1, 2))
AWAY_TAPS = ((0, 1), (0,), (4,), (3, 4))
FAR_CUTS = ((64, 160), (224, 160), (384, 32))


def kernel(
    n_lat, n_lon,
    x_ref, f_ref, s_ref, off_ref, wid_ref, halo_ref, w_hbm, out,
    ext, lines, moved, a_own, a_away, acc, conv, tail, w_ref,
    own_sem, edge_s, edge_r, near_s, near_r, far_s, far_r, lon_s, lon_r, rel_s, rel_r,
):
    rows, cols, chans = x_ref.shape
    la, lo = lax.axis_index("lat"), lax.axis_index("lon")
    west, east = lax.rem(lo + n_lon - 1, n_lon), lax.rem(lo + 1, n_lon)
    has_n, has_s = la > 0, la < n_lat - 1
    far_cuts = FAR_CUTS

    barrier = pltpu.get_barrier_semaphore()
    for lon in (west, east):
        pl.semaphore_signal(barrier, inc=1, device_id=(la, lon), device_id_type=MESH)

    @pl.when(has_n)
    def _():
        pl.semaphore_signal(barrier, inc=1, device_id=(la - 1, lo), device_id_type=MESH)

    @pl.when(has_s)
    def _():
        pl.semaphore_signal(barrier, inc=1, device_id=(la + 1, lo), device_id_type=MESH)

    own = pltpu.make_async_copy(
        x_ref, ext.at[pl.ds(HROWS, rows), pl.ds(REACH, cols)], own_sem.at[0]
    )
    own.start()
    weights = pltpu.make_async_copy(w_hbm, w_ref, own_sem.at[1])
    weights.start()

    tall = BASIS * BLOCK
    lane = lax.broadcasted_iota(jnp.int32, (BLOCK, SPAN), 1)
    step = lax.broadcasted_iota(jnp.int32, (BLOCK, SPAN), 0)
    entry = lax.broadcasted_iota(jnp.int32, (SPAN, SPAN), 0)
    place = lax.broadcasted_iota(jnp.int32, (SPAN, SPAN), 1)
    n_lines = lines.shape[0]
    line_at = lax.broadcasted_iota(jnp.int32, (n_lines, SPAN), 0)
    line_tap = (line_at - line_at // (TAPS * rows) * (TAPS * rows)) // rows

    lines[n_lines - 8:] = jnp.zeros((8, SPAN), F32)
    for k in range(BASIS):
        for t in range(TAPS):
            at = (k * TAPS + t) * rows
            lines[at:at + rows] = f_ref[k, t].astype(F32)
    for i in range(rows):
        hit = (place == entry + off_ref[i] + REACH) & (entry < wid_ref[i])
        mover = jnp.where(hit, 1.0, 0.0).astype(BF16)
        shifted = jnp.dot(lines[...].astype(BF16), mover, preferred_element_type=F32)
        moved[i] = jnp.where(jnp.abs(line_tap - HROWS) <= halo_ref[i], shifted, 0.0)

    def unit(ref, i, j, k, taps):
        at = k * BLOCK
        rest = jnp.zeros((BLOCK, SPAN), F32)
        for u, t in enumerate(taps):
            row = (k * TAPS + t) * rows + i
            line = jnp.broadcast_to(moved[i, row:row + 1], (BLOCK, SPAN))
            skew = pltpu.roll(line, 0, 1, stride=1, stride_axis=0)
            head = jnp.where(lane >= step, skew, 0.0)
            ref[j, at:at + BLOCK, u * SPAN:(u + 1) * SPAN] = head.astype(BF16)
            spot = lane - u * BLOCK
            turned = pltpu.roll(skew, u * BLOCK, 1) if u else skew
            rest = jnp.where((spot >= 0) & (spot < step), turned, rest)
        n = len(taps)
        ref[j, at:at + BLOCK, n * SPAN:(n + 1) * SPAN] = rest.astype(BF16)

    for i in range(rows):
        for k in range(BASIS):
            unit(a_own, i, i, k, OWN_TAPS[i])
            unit(a_away, i, i, k, AWAY_TAPS[i])

    peers = 2 + jnp.where(has_n, 1, 0) + jnp.where(has_s, 1, 0)
    pl.semaphore_wait(barrier, peers)

    def lat_copy(d, near, far, at, size, send, recv):
        src, dst, to = ((rows - 2, 0, la + 1), (0, rows + HROWS, la - 1))[d]
        skip, count = (0, 2) if near and far else ((1 - d, 1) if near else (d, 1))
        return pltpu.make_async_remote_copy(
            x_ref.at[pl.ds(src + skip, count), pl.ds(at, size)],
            ext.at[pl.ds(dst + skip, count), pl.ds(REACH + at, size)],
            send, recv, device_id=(to, lo), device_id_type=MESH,
        )

    def edge_copy(d, e):
        at = (0, cols - REACH)[e]
        return lat_copy(d, True, True, at, REACH, edge_s.at[d, e], edge_r.at[d, e])

    def near_copy(d):
        return lat_copy(d, True, False, REACH, cols - SPAN, near_s.at[d], near_r.at[d])

    def far_copy(d, p):
        at, size = far_cuts[p]
        return lat_copy(d, False, True, at, size, far_s.at[d, p], far_r.at[d, p])

    def lon_copy(d):
        at, to, land = ((cols - REACH, east, 0), (0, west, cols + REACH))[d]
        return pltpu.make_async_remote_copy(
            x_ref.at[:, pl.ds(at, REACH)], ext.at[pl.ds(HROWS, rows), pl.ds(land, REACH)],
            lon_s.at[d], lon_r.at[d], device_id=(la, to), device_id_type=MESH,
        )

    def relay(d, e):
        row = (0, rows + HROWS)[d]
        at, to, land = ((cols, east, 0), (REACH, west, cols + REACH))[e]
        return pltpu.make_async_remote_copy(
            ext.at[pl.ds(row, HROWS), pl.ds(at, REACH)],
            ext.at[pl.ds(row, HROWS), pl.ds(land, REACH)],
            rel_s.at[d, e], rel_r.at[d, e], device_id=(la, to), device_id_type=MESH,
        )

    sends = (has_s, has_n)
    comes = (has_n, has_s)
    pieces = range(len(far_cuts))

    def guarded(conds, action):
        for d in range(2):
            @pl.when(conds[d])
            def _():
                action(d)

    def send_edges(d):
        for e in range(2):
            edge_copy(d, e).start()

    def send_rest(d):
        near_copy(d).start()
        for p in pieces:
            far_copy(d, p).start()

    guarded(sends, send_edges)
    for d in range(2):
        lon_copy(d).start()
    guarded(sends, send_rest)

    @pl.when(jnp.logical_not(has_n))
    def _():
        ext[0:HROWS] = jnp.zeros((HROWS, cols + SPAN, chans), BF16)

    @pl.when(jnp.logical_not(has_s))
    def _():
        ext[rows + HROWS:] = jnp.zeros((HROWS, cols + SPAN, chans), BF16)

    def window(rows_in, b):
        at = b * BLOCK
        heads = [ext[r, at:at + SPAN] for r in rows_in]
        rests = [ext[r, at + SPAN:at + SPAN + BLOCK] for r in rows_in]
        return jnp.concatenate(heads + rests, 0)

    def part(ref, i, taps, b):
        depth = len(taps) * (SPAN + BLOCK)
        return jnp.dot(
            ref[i, :, 0:depth], window([i + t for t in taps], b), preferred_element_type=F32
        )

    def own_part(i, b):
        acc[i, b] = part(a_own, i, OWN_TAPS[i], b)

    def finish(i, b, ref, slot, at):
        total = acc[i, b] + part(a_away, i, AWAY_TAPS[i], b)
        for k in range(BASIS):
            scaled = total[k * BLOCK:(k + 1) * BLOCK] * s_ref[i, k]
            ref[slot, at:at + BLOCK, k * chans:(k + 1) * chans] = scaled.astype(BF16)

    blocks = cols // BLOCK
    inner = range(REACH // BLOCK, blocks - REACH // BLOCK)
    outer = [b for b in range(blocks) if b not in inner]
    own.wait()
    for b in inner:
        own_part(0, b)
        own_part(3, b)

    def pass_edges(d):
        for e in range(2):
            edge_copy(d, e).wait_recv()
        for e in range(2):
            relay(d, e).start()

    guarded(comes, pass_edges)

    for b in inner:
        own_part(1, b)
        own_part(2, b)
    for d in range(2):
        lon_copy(d).wait_recv()
    for b in outer:
        for i in range(rows):
            own_part(i, b)
    weights.wait()

    def take_corners(d):
        for e in range(2):
            relay(d, e).wait_recv()

    guarded(comes, lambda d: near_copy(d).wait_recv())
    for b in inner:
        finish(1, b, conv, 0, b * BLOCK)
        finish(2, b, conv, 1, b * BLOCK)
    guarded(comes, take_corners)
    for b in outer:
        finish(1, b, conv, 0, b * BLOCK)
        finish(2, b, conv, 1, b * BLOCK)

    def mix(ref, i, slot, at, size):
        mixed = jnp.dot(ref[slot, 0:size], w_ref[...], preferred_element_type=F32)
        out[i, at:at + size] = mixed.astype(BF16)

    size = GROUP * BLOCK
    for g in range(blocks // GROUP):
        guarded(comes, lambda d: far_copy(d, g).wait_recv())
        for u in range(GROUP):
            finish(0, g * GROUP + u, tail, 0, u * BLOCK)
            finish(3, g * GROUP + u, tail, 1, u * BLOCK)
        if g == 0:
            mix(conv, 1, 0, 0, cols)
            mix(conv, 2, 1, 0, cols)
        for slot, i in ((0, 0), (1, 3)):
            mix(tail, i, slot, g * size, size)

    def drain(d):
        for e in range(2):
            edge_copy(d, e).wait_send()
        near_copy(d).wait_send()
        for p in pieces:
            far_copy(d, p).wait_send()

    guarded(sends, drain)
    for d in range(2):
        lon_copy(d).wait_send()

    def drain_relays(d):
        for e in range(2):
            relay(d, e).wait_send()

    guarded(comes, drain_relays)


def solution(mesh):
    n_lat, n_lon = mesh.shape["lat"], mesh.shape["lon"]

    def on_device(field, filter_blocks, filter_scales, lon_offsets, lon_widths, halo_rows, mixing):
        rows, cols, chans = field.shape
        outs = mixing.shape[1]
        wide = cols + SPAN
        blocks = cols // BLOCK
        tall = BASIS * BLOCK
        n_lines = -(-BASIS * TAPS * rows // 8) * 8
        smem = pl.BlockSpec(memory_space=pltpu.SMEM)
        hbm = pl.BlockSpec(memory_space=pl.ANY)
        dma = pltpu.SemaphoreType.DMA
        filters = jnp.transpose(filter_blocks, (1, 2, 0, 3))
        return pl.pallas_call(
            functools.partial(kernel, n_lat, n_lon),
            out_shape=pltpu.VMEM((rows, cols, outs), BF16),
            in_specs=[hbm, pl.BlockSpec(memory_space=pltpu.VMEM), smem, smem, smem, smem, hbm],
            out_specs=pl.BlockSpec(memory_space=pltpu.VMEM),
            scratch_shapes=[
                pltpu.VMEM((rows + 2 * HROWS, wide, chans), BF16),
                pltpu.VMEM((n_lines, SPAN), F32),
                pltpu.VMEM((rows, n_lines, SPAN), F32),
                pltpu.VMEM((rows, tall, 5 * SPAN), BF16),
                pltpu.VMEM((rows, tall, 3 * SPAN), BF16),
                pltpu.VMEM((rows, blocks, tall, chans), F32),
                pltpu.VMEM((2, cols, BASIS * chans), BF16),
                pltpu.VMEM((2, GROUP * BLOCK, BASIS * chans), BF16),
                pltpu.VMEM((BASIS * chans, outs), BF16),
                dma((2,)),
                dma((2, 2)), dma((2, 2)),
                dma((2,)), dma((2,)),
                dma((2, len(FAR_CUTS))), dma((2, len(FAR_CUTS))),
                dma((2,)), dma((2,)),
                dma((2, 2)), dma((2, 2)),
            ],
            compiler_params=pltpu.CompilerParams(
                collective_id=0, has_side_effects=True, vmem_limit_bytes=56 * 2**20
            ),
            cost_estimate=pl.CostEstimate(
                flops=13_000_000_000, bytes_accessed=4_000_000, transcendentals=0
            ),
            name="disco",
        )(field, filters, filter_scales, lon_offsets, lon_widths, halo_rows, mixing)

    return jax.shard_map(
        on_device,
        mesh=mesh,
        in_specs=(
            P("lat", "lon", None),
            P("lat", None, None, None),
            P("lat", None),
            P("lat"),
            P("lat"),
            P("lat"),
            P(),
        ),
        out_specs=P("lat", "lon", None),
        check_vma=False,
    )
```

time: 41.4 us -> 31.8 us (0.77)
  the two profiles are of different devices: /device:TPU:193 before, /device:TPU:161 now
where the time goes in v2:
time: 31.8 us; the launch traced here: 31.7 us
  Pallas kernels  30.7 us (97%)
  local copies, waits for them, and re-layouts  0.95 us (3%)
    pallas_call x1, Pallas kernels, on_device(): pl.pallas_call(functools.partial(kernel, n_lat, n_lon), out_shape=pltpu.V...  30.7 us
    unnamed x1, local copies, waits for them, and re-layouts  0.95 us

profile of v2, /device:TPU:161, one launch (start us, length us, event | category | flops | bytes accessed | tf_op | source)
XLA Modules:
  0.0 31.7 jit_solution(5246061347935849441)
XLA Ops:
  0.0 30.7 %disco.1 = bf16[4,480,256]{2,1,0:T(8,128)(2,1)S(1)} custom-call(bf16[4,480,256]{2,1,0:T(8,128)(2,1)} %x_ref.1, bf16[9,5,4,128]{3,2,1,0:T(4,128)(2,1)} %bitcast.1, f32[4,9]{1,0:T(4,128)} %s_ref.1, s32[4]{0:T(128)} %off_ref.1, s32[4]{0:T(128)} %wid_ref.1, s32[4]{0:T(128)} %halo_ref.1, bf16[2304,256]{1,0:T(8,128)(2,1)} %w_hbm.1), custom_call_target="tpu_custom_call" | custom-call | flops 12999999488 | bytes 4000000 | tf_op jit(solution)/shard_map/disco/pallas_call | solution.py:276
  30.7 0.9 %copy.9 = bf16[4,480,256]{2,1,0:T(8,128)(2,1)} copy(bf16[4,480,256]{2,1,0:T(8,128)(2,1)S(1)} %disco.1) | data formatting | bytes 1966080

commit v3 on v2

--- a/solution.py
+++ b/solution.py
@@ -14,19 +14,19 @@
 REACH = 64
 SPAN = 2 * REACH
 BLOCK = 32
-GROUP = 5
 F32 = jnp.float32
 BF16 = jnp.bfloat16
 
 OWN_TAPS = ((2, 3, 4), (1, 2, 3, 4), (0, 1, 2, 3), (0, 1, 2))
 AWAY_TAPS = ((0, 1), (0,), (4,), (3, 4))
 FAR_CUTS = ((64, 160), (224, 160), (384, 32))
+STAGES = ((2, 5), (5, 10), (10, 15))
 
 
 def kernel(
     n_lat, n_lon,
     x_ref, f_ref, s_ref, off_ref, wid_ref, halo_ref, w_hbm, out,
-    ext, lines, moved, a_own, a_away, acc, conv, tail, w_ref,
+    ext, lines, moved, a_own, a_away, acc, conv, tail, edge, w_ref,
     own_sem, edge_s, edge_r, near_s, near_r, far_s, far_r, lon_s, lon_r, rel_s, rel_r,
 ):
     rows, cols, chans = x_ref.shape
@@ -143,19 +143,13 @@
             def _():
                 action(d)
 
-    def send_edges(d):
-        for e in range(2):
-            edge_copy(d, e).start()
-
-    def send_rest(d):
-        near_copy(d).start()
-        for p in pieces:
-            far_copy(d, p).start()
-
-    guarded(sends, send_edges)
     for d in range(2):
         lon_copy(d).start()
-    guarded(sends, send_rest)
+    for e in range(2):
+        guarded(sends, lambda d: edge_copy(d, e).start())
+    guarded(sends, lambda d: near_copy(d).start())
+    for p in pieces:
+        guarded(sends, lambda d: far_copy(d, p).start())
 
     @pl.when(jnp.logical_not(has_n))
     def _():
@@ -180,11 +174,11 @@
     def own_part(i, b):
         acc[i, b] = part(a_own, i, OWN_TAPS[i], b)
 
-    def finish(i, b, ref, slot, at):
+    def finish(i, b, ref, at):
         total = acc[i, b] + part(a_away, i, AWAY_TAPS[i], b)
         for k in range(BASIS):
             scaled = total[k * BLOCK:(k + 1) * BLOCK] * s_ref[i, k]
-            ref[slot, at:at + BLOCK, k * chans:(k + 1) * chans] = scaled.astype(BF16)
+            ref[at:at + BLOCK, k * chans:(k + 1) * chans] = scaled.astype(BF16)
 
     blocks = cols // BLOCK
     inner = range(REACH // BLOCK, blocks - REACH // BLOCK)
@@ -193,53 +187,71 @@
     for b in inner:
         own_part(0, b)
         own_part(3, b)
-
-    def pass_edges(d):
-        for e in range(2):
-            edge_copy(d, e).wait_recv()
-        for e in range(2):
-            relay(d, e).start()
-
-    guarded(comes, pass_edges)
-
     for b in inner:
         own_part(1, b)
         own_part(2, b)
+
+    def pass_edges(d):
+        for e in range(2):
+            edge_copy(d, e).wait_recv()
+        for e in range(2):
+            relay(d, e).start()
+
+    guarded(comes, pass_edges)
+    weights.wait()
+    guarded(comes, lambda d: near_copy(d).wait_recv())
+    n_in = len(inner) * BLOCK
+    for n, b in enumerate(inner):
+        finish(1, b, conv, n * BLOCK)
+        finish(2, b, conv, n_in + n * BLOCK)
+
+    def mix(ref, at, size, lands):
+        mixed = jnp.dot(ref[at:at + size], w_ref[...], preferred_element_type=F32).astype(BF16)
+        at = 0
+        for i, b, count in lands:
+            out[i, b * BLOCK:(b + count) * BLOCK] = mixed[at:at + count * BLOCK]
+            at += count * BLOCK
+
+    def take_corners(d):
+        for e in range(2):
+            relay(d, e).wait_recv()
+
+    for g, (lo_b, hi_b) in enumerate(STAGES[:-1]):
+        guarded(comes, lambda d: far_copy(d, g).wait_recv())
+        count = hi_b - lo_b
+        for b in range(lo_b, hi_b):
+            finish(0, b, tail, (b - lo_b) * BLOCK)
+            finish(3, b, tail, (count + b - lo_b) * BLOCK)
+        if g == 0:
+            mix(conv, 0, n_in, [(1, inner[0], len(inner))])
+            mix(conv, n_in, n_in, [(2, inner[0], len(inner))])
+        for n, i in enumerate((0, 3)):
+            mix(tail, n * count * BLOCK, count * BLOCK, [(i, lo_b, count)])
+
     for d in range(2):
         lon_copy(d).wait_recv()
     for b in outer:
         for i in range(rows):
             own_part(i, b)
-    weights.wait()
-
-    def take_corners(d):
-        for e in range(2):
-            relay(d, e).wait_recv()
-
-    guarded(comes, lambda d: near_copy(d).wait_recv())
-    for b in inner:
-        finish(1, b, conv, 0, b * BLOCK)
-        finish(2, b, conv, 1, b * BLOCK)
+
     guarded(comes, take_corners)
-    for b in outer:
-        finish(1, b, conv, 0, b * BLOCK)
-        finish(2, b, conv, 1, b * BLOCK)
-
-    def mix(ref, i, slot, at, size):
-        mixed = jnp.dot(ref[slot, 0:size], w_ref[...], preferred_element_type=F32)
-        out[i, at:at + size] = mixed.astype(BF16)
-
-    size = GROUP * BLOCK
-    for g in range(blocks // GROUP):
-        guarded(comes, lambda d: far_copy(d, g).wait_recv())
-        for u in range(GROUP):
-            finish(0, g * GROUP + u, tail, 0, u * BLOCK)
-            finish(3, g * GROUP + u, tail, 1, u * BLOCK)
-        if g == 0:
-            mix(conv, 1, 0, 0, cols)
-            mix(conv, 2, 1, 0, cols)
-        for slot, i in ((0, 0), (1, 3)):
-            mix(tail, i, slot, g * size, size)
+    for n, b in enumerate(outer):
+        finish(1, b, edge, n * BLOCK)
+        finish(2, b, edge, (len(outer) + n) * BLOCK)
+    guarded(comes, lambda d: far_copy(d, len(STAGES) - 1).wait_recv())
+    lo_b, hi_b = STAGES[-1]
+    ends = list(range(lo_b, hi_b)) + list(range(inner[0]))
+    base = 2 * len(outer)
+    for n, b in enumerate(ends):
+        finish(0, b, edge, (base + n) * BLOCK)
+        finish(3, b, edge, (base + len(ends) + n) * BLOCK)
+    for n, i in enumerate((1, 2)):
+        side = inner[0]
+        mix(edge, n * len(outer) * BLOCK, len(outer) * BLOCK,
+            [(i, 0, side), (i, blocks - side, side)])
+    for n, i in enumerate((0, 3)):
+        mix(edge, (base + n * len(ends)) * BLOCK, len(ends) * BLOCK,
+            [(i, lo_b, hi_b - lo_b), (i, 0, inner[0])])
 
     def drain(d):
         for e in range(2):
@@ -285,8 +297,9 @@
                 pltpu.VMEM((rows, tall, 5 * SPAN), BF16),
                 pltpu.VMEM((rows, tall, 3 * SPAN), BF16),
                 pltpu.VMEM((rows, blocks, tall, chans), F32),
-                pltpu.VMEM((2, cols, BASIS * chans), BF16),
-                pltpu.VMEM((2, GROUP * BLOCK, BASIS * chans), BF16),
+                pltpu.VMEM((2 * (cols - SPAN), BASIS * chans), BF16),
+                pltpu.VMEM((2 * 5 * BLOCK, BASIS * chans), BF16),
+                pltpu.VMEM((22 * BLOCK, BASIS * chans), BF16),
                 pltpu.VMEM((BASIS * chans, outs), BF16),
                 dma((2,)),
                 dma((2, 2)), dma((2, 2)),

time: 31.8 us -> 30.3 us (0.953)
  the two profiles are of different devices: /device:TPU:161 before, /device:TPU:198 now
where the time goes in v3:
time: 30.3 us; the launch traced here: 30.2 us
  Pallas kernels  29.2 us (96%)
  local copies, waits for them, and re-layouts  0.95 us (3%)
    pallas_call x1, Pallas kernels, on_device(): pl.pallas_call(functools.partial(kernel, n_lat, n_lon), out_shape=pltpu.V...  29.2 us
    unnamed x1, local copies, waits for them, and re-layouts  0.95 us

profile of v3, /device:TPU:198, one launch (start us, length us, event | category | flops | bytes accessed | tf_op | source)
XLA Modules:
  0.0 30.2 jit_solution(16667920797797828161)
XLA Ops:
  0.0 29.2 %disco.1 = bf16[4,480,256]{2,1,0:T(8,128)(2,1)S(1)} custom-call(bf16[4,480,256]{2,1,0:T(8,128)(2,1)} %x_ref.1, bf16[9,5,4,128]{3,2,1,0:T(4,128)(2,1)} %bitcast.1, f32[4,9]{1,0:T(4,128)} %s_ref.1, s32[4]{0:T(128)} %off_ref.1, s32[4]{0:T(128)} %wid_ref.1, s32[4]{0:T(128)} %halo_ref.1, bf16[2304,256]{1,0:T(8,128)(2,1)} %w_hbm.1), custom_call_target="tpu_custom_call" | custom-call | flops 12999999488 | bytes 4000000 | tf_op jit(solution)/shard_map/disco/pallas_call | solution.py:288
  29.3 0.9 %copy.9 = bf16[4,480,256]{2,1,0:T(8,128)(2,1)} copy(bf16[4,480,256]{2,1,0:T(8,128)(2,1)S(1)} %disco.1) | data formatting | bytes 1966080

commit v4 on v3

--- a/solution.py
+++ b/solution.py
@@ -235,23 +235,21 @@
             own_part(i, b)
 
     guarded(comes, take_corners)
+    side = inner[0]
+    lo_b, hi_b = STAGES[-1]
+    ends = list(range(lo_b, hi_b)) + list(range(side))
+    base = len(outer)
+    half = (base + len(ends)) * BLOCK
     for n, b in enumerate(outer):
         finish(1, b, edge, n * BLOCK)
-        finish(2, b, edge, (len(outer) + n) * BLOCK)
+        finish(2, b, edge, half + n * BLOCK)
     guarded(comes, lambda d: far_copy(d, len(STAGES) - 1).wait_recv())
-    lo_b, hi_b = STAGES[-1]
-    ends = list(range(lo_b, hi_b)) + list(range(inner[0]))
-    base = 2 * len(outer)
     for n, b in enumerate(ends):
         finish(0, b, edge, (base + n) * BLOCK)
-        finish(3, b, edge, (base + len(ends) + n) * BLOCK)
-    for n, i in enumerate((1, 2)):
-        side = inner[0]
-        mix(edge, n * len(outer) * BLOCK, len(outer) * BLOCK,
-            [(i, 0, side), (i, blocks - side, side)])
-    for n, i in enumerate((0, 3)):
-        mix(edge, (base + n * len(ends)) * BLOCK, len(ends) * BLOCK,
-            [(i, lo_b, hi_b - lo_b), (i, 0, inner[0])])
+        finish(3, b, edge, half + (base + n) * BLOCK)
+    for at, i, j in ((0, 1, 0), (half, 2, 3)):
+        mix(edge, at, half,
+            [(i, 0, side), (i, blocks - side, side), (j, lo_b, hi_b - lo_b), (j, 0, side)])
 
     def drain(d):
         for e in range(2):

time: 30.3 us -> 30.3 us (level)
  no operation moved by 1% of the time
where the time goes in v4:
time: 30.3 us; the launch traced here: 30.2 us
  Pallas kernels  29.2 us (96%)
  local copies, waits for them, and re-layouts  0.95 us (3%)
    pallas_call x1, Pallas kernels, on_device(): pl.pallas_call(functools.partial(kernel, n_lat, n_lon), out_shape=pltpu.V...  29.2 us
    unnamed x1, local copies, waits for them, and re-layouts  0.95 us

profile of v4, /device:TPU:198, one launch (start us, length us, event | category | flops | bytes accessed | tf_op | source)
XLA Modules:
  0.0 30.2 jit_solution(5666370240662046323)
XLA Ops:
  0.0 29.2 %disco.1 = bf16[4,480,256]{2,1,0:T(8,128)(2,1)S(1)} custom-call(bf16[4,480,256]{2,1,0:T(8,128)(2,1)} %x_ref.1, bf16[9,5,4,128]{3,2,1,0:T(4,128)(2,1)} %bitcast.1, f32[4,9]{1,0:T(4,128)} %s_ref.1, s32[4]{0:T(128)} %off_ref.1, s32[4]{0:T(128)} %wid_ref.1, s32[4]{0:T(128)} %halo_ref.1, bf16[2304,256]{1,0:T(8,128)(2,1)} %w_hbm.1), custom_call_target="tpu_custom_call" | custom-call | flops 12999999488 | bytes 4000000 | tf_op jit(solution)/shard_map/disco/pallas_call | solution.py:286
  29.2 0.9 %copy.9 = bf16[4,480,256]{2,1,0:T(8,128)(2,1)} copy(bf16[4,480,256]{2,1,0:T(8,128)(2,1)S(1)} %disco.1) | data formatting | bytes 1966080

commit v5 on v4

--- a/solution.py
+++ b/solution.py
@@ -187,17 +187,19 @@
     for b in inner:
         own_part(0, b)
         own_part(3, b)
+
+    def pass_edges(d):
+        for e in range(2):
+            edge_copy(d, e).wait_recv()
+        for e in range(2):
+            relay(d, e).start()
+
+    guarded(comes, pass_edges)
+
     for b in inner:
         own_part(1, b)
         own_part(2, b)
 
-    def pass_edges(d):
-        for e in range(2):
-            edge_copy(d, e).wait_recv()
-        for e in range(2):
-            relay(d, e).start()
-
-    guarded(comes, pass_edges)
     weights.wait()
     guarded(comes, lambda d: near_copy(d).wait_recv())
     n_in = len(inner) * BLOCK

time: 30.3 us -> 30.3 us (level)
  no operation moved by 1% of the time
where the time goes in v5:
time: 30.3 us; the launch traced here: 30.2 us
  Pallas kernels  29.2 us (96%)
  local copies, waits for them, and re-layouts  0.95 us (3%)
    pallas_call x1, Pallas kernels, on_device(): pl.pallas_call(functools.partial(kernel, n_lat, n_lon), out_shape=pltpu.V...  29.2 us
    unnamed x1, local copies, waits for them, and re-layouts  0.95 us

profile of v5, /device:TPU:198, one launch (start us, length us, event | category | flops | bytes accessed | tf_op | source)
XLA Modules:
  0.0 30.2 jit_solution(3434863588212758059)
XLA Ops:
  0.0 29.2 %disco.1 = bf16[4,480,256]{2,1,0:T(8,128)(2,1)S(1)} custom-call(bf16[4,480,256]{2,1,0:T(8,128)(2,1)} %x_ref.1, bf16[9,5,4,128]{3,2,1,0:T(4,128)(2,1)} %bitcast.1, f32[4,9]{1,0:T(4,128)} %s_ref.1, s32[4]{0:T(128)} %off_ref.1, s32[4]{0:T(128)} %wid_ref.1, s32[4]{0:T(128)} %halo_ref.1, bf16[2304,256]{1,0:T(8,128)(2,1)} %w_hbm.1), custom_call_target="tpu_custom_call" | custom-call | flops 12999999488 | bytes 4000000 | tf_op jit(solution)/shard_map/disco/pallas_call | solution.py:288
  29.2 0.9 %copy.9 = bf16[4,480,256]{2,1,0:T(8,128)(2,1)} copy(bf16[4,480,256]{2,1,0:T(8,128)(2,1)S(1)} %disco.1) | data formatting | bytes 1966080
